TPU v7x, 32 devices: a whole 2x2x4 slice. The times are simulated.
32 devices in a mesh: fsdp: 32 (over z, y, x, core).
Axes of the slice: x: 2, y: 2, z: 4, core: 2. Of those that a mesh axis runs over, the one named last changes fastest.
Arguments:
- inputs: bfloat16 [16384, 1024], P('fsdp'), may hold values from -6 to 6
- seq_lens: int32 [32, 8], P('fsdp'), may hold values from 0 to 512, as said below
- mixer_gain: bfloat16 [1024], P('fsdp'), may hold values from 0.5 to 1.5
- input_proj: bfloat16 [1024, 3072], P('fsdp'), may hold values from -0.1875 to 0.1875
- conv_taps: bfloat16 [3072, 4], P('fsdp'), may hold values from -3 to 3
- rate_proj: bfloat16 [1024, 12], P('fsdp'), may hold values from -0.1875 to 0.1875
- decay_params: float32 [2, 6], replicated, may hold values from -6.5 to 1, as said below
- outgate_proj: bfloat16 [1024, 1536], P('fsdp'), may hold values from -0.1875 to 0.1875
- head_gain: float32 [256], replicated, may hold values from 0.5 to 1.5
- output_proj: bfloat16 [1536, 1024], P('fsdp'), may hold values from -0.15625 to 0.15625
- feed_gain: bfloat16 [1024], P('fsdp'), may hold values from 0.5 to 1.5
- gate_proj: bfloat16 [1024, 2816], P('fsdp'), may hold values from -0.1875 to 0.1875
- up_proj: bfloat16 [1024, 2816], P('fsdp'), may hold values from -0.1875 to 0.1875
- down_proj: bfloat16 [2816, 1024], P('fsdp'), may hold values from -0.109375 to 0.109375
- cotangent: bfloat16 [16384, 1024], P('fsdp'), may hold values from -6 to 6
Outputs:
- output: bfloat16 [16384, 1024], P('fsdp')
- grad_inputs: float32 [16384, 1024], P('fsdp')
- grad_mixer_gain: float32 [1024], P('fsdp')
- grad_input_proj: float32 [1024, 3072], P('fsdp')
- grad_conv_taps: float32 [3072, 4], P('fsdp')
- grad_rate_proj: float32 [1024, 12], P('fsdp')
- grad_decay_params: float32 [2, 6], replicated
- grad_outgate_proj: float32 [1024, 1536], P('fsdp')
- grad_head_gain: float32 [256], replicated
- grad_output_proj: float32 [1536, 1024], P('fsdp')
- grad_feed_gain: float32 [1024], P('fsdp')
- grad_gate_proj: float32 [1024, 2816], P('fsdp')
- grad_up_proj: float32 [1024, 2816], P('fsdp')
- grad_down_proj: float32 [2816, 1024], P('fsdp')
Inputs may be any that keep to these rules, and one draw needn't show every extreme that they name: `seq_lens`: row d lists the lengths of the sequences on device d in the order in which they lie, nonzero entries first and zeros after them. Each device's lengths, each rounded up to a multiple of 64, add up to at most 512, and on some device to exactly 512; some sequence has exactly 512 tokens. `decay_params`: row 0 holds each head's logarithm of the decay scale, row 1 its decay bias.
All inputs are finite; a program needn't handle non-finite values.
Results may differ from a plain program's by a relative error of at most 0.02.
The roundings to bfloat16 on the way count: a program that leaves them out, or rounds other values in their place, can miss the bound.
Values may be sent and summed in bfloat16 or wider, within the bound.
A program may use at most 256 MiB of HBM per device.

v0:
```python
import jax
import jax.numpy as jnp
from jax import lax
from jax.sharding import PartitionSpec as P

NH = 6
DK = 128
DV = 256
CONV = 4
GROUP = 64


EPS = 1e-06
TRIPLE = lax.Precision.HIGH


def rms_norm(values, norm_gain):
    return values * lax.rsqrt(jnp.mean(values * values, axis=-1, keepdims=True) + EPS) * norm_gain


def layout(lengths, row_count):
    padded = (lengths + GROUP - 1) // GROUP * GROUP
    starts = jnp.cumsum(padded) - padded
    offset = jnp.arange(row_count, dtype=jnp.int32)[:, None] - starts[None, :]
    inside = (offset >= 0) & (offset < padded[None, :])
    live_rows = jnp.sum(jnp.where(inside & (offset < lengths[None, :]), 1.0, 0.0), axis=1).astype(
        jnp.float32
    )
    position = jnp.sum(jnp.where(inside, offset, 0), axis=1)
    return (live_rows, position)


def short_conv(mixed_rows, tap_values, position):
    summed = mixed_rows * tap_values[:, CONV - 1]
    for distance in range(1, CONV):
        shifted = jnp.concatenate(
            [jnp.zeros((distance, mixed_rows.shape[1]), mixed_rows.dtype), mixed_rows[:-distance]],
            axis=0,
        )
        summed = (
            summed
            + jnp.where((position >= distance)[:, None], shifted, 0.0)
            * tap_values[:, CONV - 1 - distance]
        )
    return summed


def qkv_heads(mixed_rows, tap_values, position):
    row_count = mixed_rows.shape[0]
    activated = jax.nn.silu(short_conv(mixed_rows, tap_values, position))
    queries = activated[:, : NH * DK].reshape(row_count, NH, DK)
    keys = activated[:, NH * DK : 2 * NH * DK].reshape(row_count, NH, DK)
    values = activated[:, 2 * NH * DK :].reshape(row_count, NH, DV)
    queries = (
        queries * lax.rsqrt(jnp.sum(queries * queries, axis=-1, keepdims=True) + EPS) * DK ** (-0.5)
    )
    keys = keys * lax.rsqrt(jnp.sum(keys * keys, axis=-1, keepdims=True) + EPS)
    return (queries, keys, values)


def gates(rate_logits, decay_params, live_rows):
    write_rate = jax.nn.sigmoid(rate_logits[:, :NH]) * live_rows[:, None]
    log_decay = (
        -jnp.exp(decay_params[0])
        * jax.nn.softplus(rate_logits[:, NH:] + decay_params[1])
        * live_rows[:, None]
    )
    return (write_rate, log_decay)


def group_step(state, block):
    queries, keys, values, write_rate, log_decay, restart = block
    state = state * (1.0 - restart)
    block_len = queries.shape[0]
    total_decay = jnp.cumsum(log_decay, axis=0)
    lower = jnp.tril(jnp.ones((block_len, block_len), jnp.float32))
    identity = jnp.eye(block_len, dtype=jnp.float32)
    strict = lower - identity
    gaps = total_decay.T[:, :, None] - total_decay.T[:, None, :]
    within = jnp.exp(jnp.where(lower > 0, gaps, 0.0)) * lower
    key_key = jnp.einsum("thd,ihd->hti", keys, keys, precision=TRIPLE)
    coupling = write_rate.T[:, :, None] * within * key_key * strict
    start_key = jnp.einsum("thd,hde->hte", keys, state, precision=TRIPLE)
    scaled = (write_rate * jnp.exp(total_decay)).T[:, :, None]
    target = write_rate.T[:, :, None] * values.transpose(1, 0, 2) - scaled * start_key
    pseudo = jax.scipy.linalg.solve_triangular(identity + coupling, target, lower=True)
    query_key = jnp.einsum("thd,ihd->hti", queries, keys, precision=TRIPLE) * within
    start_query = jnp.einsum("thd,hde->hte", queries, state, precision=TRIPLE)
    outputs = jnp.exp(total_decay).T[:, :, None] * start_query + jnp.einsum(
        "hti,hie->hte", query_key, pseudo, precision=TRIPLE
    )
    tail_decay = jnp.exp(total_decay[-1][None, :] - total_decay)
    state = jnp.exp(total_decay[-1])[:, None, None] * state + jnp.einsum(
        "ihd,ih,hie->hde", keys, tail_decay, pseudo, precision=TRIPLE
    )
    return (state, outputs.transpose(1, 0, 2))


def delta_rule(queries, keys, values, write_rate, log_decay, position):
    row_count = queries.shape[0]
    blocks = row_count // GROUP

    def to_blocks(array):
        return array.reshape((blocks, GROUP) + array.shape[1:])

    restart = jnp.where(position.reshape(blocks, GROUP)[:, 0] == 0, 1.0, 0.0).astype(jnp.float32)
    initial = jnp.zeros((NH, DK, DV), jnp.float32)
    last_state, outputs = lax.scan(
        jax.checkpoint(group_step),
        initial,
        (
            to_blocks(queries),
            to_blocks(keys),
            to_blocks(values),
            to_blocks(write_rate),
            to_blocks(log_decay),
            restart,
        ),
    )
    return outputs.reshape(row_count, NH, DV)


def mixer_core(queries, keys, values, rate_logits, decay_params, live_rows, position):
    write_rate, log_decay = gates(rate_logits, decay_params, live_rows)
    return delta_rule(queries, keys, values, write_rate, log_decay, position)


def gated_norm(recurrent, gate_logits, head_gain):
    row_count = recurrent.shape[0]
    return rms_norm(recurrent, head_gain) * jax.nn.silu(gate_logits.reshape(row_count, NH, DV))


def rounded(values):
    return lax.optimization_barrier(values.astype(jnp.bfloat16)).astype(jnp.float32)


def swiglu(gate_in, up_in):
    return jax.nn.silu(gate_in) * up_in


def side_by_side(members):
    return jnp.concatenate(
        [member if member.ndim == 2 else member[:, None] for member in members], axis=1
    )


def split_columns(joined, members):
    pieces = []
    column = 0
    for member in members:
        width = member.shape[1] if member.ndim == 2 else 1
        piece = joined[:, column : column + width]
        pieces.append(piece if member.ndim == 2 else piece[:, 0])
        column = column + width
    return pieces


def by_owner(members, owners):
    width = members[0].shape[1]
    return jnp.concatenate(
        [member.reshape(owners, -1, width) for member in members], axis=1
    ).reshape(-1, width)


def split_rows(joined, members, owners):
    pieces = []
    first = 0
    for member in members:
        height = member.shape[0] // owners
        pieces.append(joined[first : first + height])
        first = first + height
    return pieces


def shards(
    inputs,
    seq_lens,
    mixer_gain,
    input_proj,
    conv_taps,
    rate_proj,
    decay_params,
    outgate_proj,
    head_gain,
    output_proj,
    feed_gain,
    gate_proj,
    up_proj,
    down_proj,
    cotangent,
):
    row_count = inputs.shape[0]
    owners = lax.axis_size("fsdp")
    live_rows, position = layout(seq_lens[0], row_count)
    gathered = (
        lax.all_gather(mixer_gain, "fsdp", axis=0, tiled=True),
        lax.all_gather(input_proj, "fsdp", axis=0, tiled=True),
        lax.all_gather(conv_taps, "fsdp", axis=0, tiled=True),
        lax.all_gather(rate_proj, "fsdp", axis=0, tiled=True),
        lax.all_gather(outgate_proj, "fsdp", axis=0, tiled=True),
        lax.all_gather(output_proj, "fsdp", axis=0, tiled=True),
        lax.all_gather(feed_gain, "fsdp", axis=0, tiled=True),
        lax.all_gather(gate_proj, "fsdp", axis=0, tiled=True),
        lax.all_gather(up_proj, "fsdp", axis=0, tiled=True),
        lax.all_gather(down_proj, "fsdp", axis=0, tiled=True),
    )
    (
        full_mgain,
        full_in,
        full_taps,
        full_rate,
        full_outgate,
        full_out,
        full_fgain,
        full_gate,
        full_up,
        full_down,
    ) = gathered
    stream = inputs.astype(jnp.float32)
    normed_wide, norm_one_back = jax.vjp(rms_norm, stream, full_mgain.astype(jnp.float32))
    normed = normed_wide.astype(jnp.bfloat16)
    mixed_in = jnp.dot(normed, full_in, preferred_element_type=jnp.float32)
    rate_logits = jnp.dot(normed, full_rate, preferred_element_type=jnp.float32)
    gate_logits = jnp.dot(normed, full_outgate, preferred_element_type=jnp.float32)

    def heads_fn(mixed_rows, tap_values):
        return qkv_heads(mixed_rows, tap_values, position)

    (queries, keys, values), heads_back = jax.vjp(heads_fn, mixed_in, full_taps.astype(jnp.float32))

    def core_fn(query_in, key_in, value_in, rate_in, param_in):
        return mixer_core(query_in, key_in, value_in, rate_in, param_in, live_rows, position)

    recurrent, core_back = jax.vjp(
        core_fn, rounded(queries), rounded(keys), rounded(values), rate_logits, decay_params
    )
    head_normed, head_back = jax.vjp(gated_norm, recurrent, gate_logits, head_gain)
    head_out = head_normed.reshape(row_count, NH * DV).astype(jnp.bfloat16)
    middle = stream + jnp.dot(head_out, full_out, preferred_element_type=jnp.float32)
    normed_two_wide, norm_two_back = jax.vjp(rms_norm, middle, full_fgain.astype(jnp.float32))
    normed_two = normed_two_wide.astype(jnp.bfloat16)
    gate_act = jnp.dot(normed_two, full_gate, preferred_element_type=jnp.float32)
    up_act = jnp.dot(normed_two, full_up, preferred_element_type=jnp.float32)
    hidden_wide, swiglu_back = jax.vjp(swiglu, gate_act, up_act)
    hidden = hidden_wide.astype(jnp.bfloat16)
    output = (
        (middle + jnp.dot(hidden, full_down, preferred_element_type=jnp.float32))
        * live_rows[:, None]
    ).astype(jnp.bfloat16)
    regathered = (
        lax.all_gather(input_proj, "fsdp", axis=0, tiled=True),
        lax.all_gather(rate_proj, "fsdp", axis=0, tiled=True),
        lax.all_gather(outgate_proj, "fsdp", axis=0, tiled=True),
        lax.all_gather(output_proj, "fsdp", axis=0, tiled=True),
        lax.all_gather(gate_proj, "fsdp", axis=0, tiled=True),
        lax.all_gather(up_proj, "fsdp", axis=0, tiled=True),
        lax.all_gather(down_proj, "fsdp", axis=0, tiled=True),
    )
    back_in, back_rate, back_outgate, back_out, back_gate, back_up, back_down = regathered
    d_final = cotangent.astype(jnp.float32) * live_rows[:, None]
    d_ffn = d_final.astype(jnp.bfloat16)
    grad_down = jnp.einsum("rf,rd->fd", hidden, d_ffn, preferred_element_type=jnp.float32)
    d_hidden = jnp.einsum("rd,fd->rf", d_ffn, back_down, preferred_element_type=jnp.float32)
    d_gate_wide, d_up_wide = swiglu_back(d_hidden)
    d_gate = d_gate_wide.astype(jnp.bfloat16)
    d_up = d_up_wide.astype(jnp.bfloat16)
    grad_gate = jnp.einsum("rd,rf->df", normed_two, d_gate, preferred_element_type=jnp.float32)
    grad_up = jnp.einsum("rd,rf->df", normed_two, d_up, preferred_element_type=jnp.float32)
    d_normed_two = jnp.einsum(
        "rf,df->rd", d_gate, back_gate, preferred_element_type=jnp.float32
    ) + jnp.einsum("rf,df->rd", d_up, back_up, preferred_element_type=jnp.float32)
    d_middle_part, grad_fgain = norm_two_back(d_normed_two)
    d_middle = d_final + d_middle_part
    feed_members = (grad_fgain, grad_gate, grad_up)
    d_branch = d_middle.astype(jnp.bfloat16)
    grad_out = jnp.einsum("rv,rd->vd", head_out, d_branch, preferred_element_type=jnp.float32)
    d_head = jnp.einsum(
        "rd,vd->rv", d_branch, back_out, preferred_element_type=jnp.float32
    ).reshape(row_count, NH, DV)
    d_recurrent, d_gate_logits, grad_hgain = head_back(d_head)
    d_queries, d_keys, d_values, d_rates, grad_dparams = core_back(d_recurrent)
    d_mixed, grad_taps = heads_back((d_queries, d_keys, d_values))
    d_mixed_low = d_mixed.astype(jnp.bfloat16)
    d_rates_low = d_rates.astype(jnp.bfloat16)
    d_outgate_low = d_gate_logits.astype(jnp.bfloat16)
    grad_in = jnp.einsum("rd,rc->dc", normed, d_mixed_low, preferred_element_type=jnp.float32)
    grad_rate = jnp.einsum("rd,rc->dc", normed, d_rates_low, preferred_element_type=jnp.float32)
    grad_outgate = jnp.einsum(
        "rd,rc->dc", normed, d_outgate_low, preferred_element_type=jnp.float32
    )
    d_normed = jnp.einsum("rc,dc->rd", d_mixed_low, back_in, preferred_element_type=jnp.float32)
    d_normed = d_normed + jnp.einsum(
        "rc,dc->rd", d_rates_low, back_rate, preferred_element_type=jnp.float32
    )
    d_normed = d_normed + jnp.einsum(
        "rc,dc->rd", d_outgate_low, back_outgate, preferred_element_type=jnp.float32
    )
    d_stream, grad_mgain = norm_one_back(d_normed)
    grad_inputs = d_middle + d_stream
    small_sums = lax.psum((grad_dparams, grad_hgain, grad_taps), "fsdp")
    tap_rows = grad_taps.shape[0] // owners
    taps_mine = lax.dynamic_slice_in_dim(
        small_sums[2], lax.axis_index("fsdp") * tap_rows, tap_rows, 0
    )
    mixer_members = (grad_mgain, grad_in, grad_rate, grad_outgate)
    wide_joined = side_by_side(mixer_members + feed_members)
    wide_mine = lax.psum_scatter(wide_joined, "fsdp", scatter_dimension=0, tiled=True)
    tall_members = (grad_out, grad_down)
    tall_joined = by_owner(tall_members, owners)
    tall_mine = lax.psum_scatter(tall_joined, "fsdp", scatter_dimension=0, tiled=True)
    mgain_mine, in_mine, rate_mine, outgate_mine, fgain_mine, gate_mine, up_mine = split_columns(
        wide_mine, mixer_members + feed_members
    )
    out_mine, down_mine = split_rows(tall_mine, tall_members, owners)
    return (
        output,
        grad_inputs,
        mgain_mine,
        in_mine,
        taps_mine,
        rate_mine,
        small_sums[0],
        outgate_mine,
        small_sums[1],
        out_mine,
        fgain_mine,
        gate_mine,
        up_mine,
        down_mine,
    )


def solution(mesh):
    placed = (
        P("fsdp", None),
        P("fsdp", None),
        P("fsdp"),
        P("fsdp", None),
        P("fsdp", None),
        P("fsdp", None),
        P(),
        P("fsdp", None),
        P(),
        P("fsdp", None),
        P("fsdp"),
        P("fsdp", None),
        P("fsdp", None),
        P("fsdp", None),
        P("fsdp", None),
    )
    return jax.shard_map(
        shards,
        mesh=mesh,
        in_specs=placed,
        out_specs=(
            P("fsdp", None),
            P("fsdp", None),
            P("fsdp"),
            P("fsdp", None),
            P("fsdp", None),
            P("fsdp", None),
            P(),
            P("fsdp", None),
            P(),
            P("fsdp", None),
            P("fsdp"),
            P("fsdp", None),
            P("fsdp", None),
            P("fsdp", None),
        ),
        check_vma=False,
    )
```

profile of v0, /device:TPU:0, one launch (start us, length us, event | category | flops | bytes accessed | tf_op | source)
XLA Modules:
  0.0 1663.4 jit_solution(13858571092286549091)
XLA Ops:
  15.1 44.3 %all-gather = bf16[32,32,12]{1,2,0:T(8,128)(2,1)S(1)} all-gather(bf16[1,32,12]{1,2,0:T(8,128)(2,1)} %bitcast.577), channel_id=1, replica_groups=mesh['fsdp'=32] {'fsdp'}, dimensions={0}, use_global_device_ids=true | all-gather | bytes 25344 | tf_op jit(solution)/shard_map/all_gather | solution.py:199
  61.2 38.2 %all-reduce.22 = (bf16[1024]{0:T(1024)(128)(2,1)S(1)}, bf16[1024]{0:T(1024)(128)(2,1)S(1)}) all-reduce(bf16[1024]{0:T(1024)(128)(2,1)S(1)} %dynamic-update-slice, bf16[1024]{0:T(1024)(128)(2,1)S(1)} %dynamic-update-slice.1), channel_id=1, replica_groups=mesh['fsdp'=32] {'fsdp'}, use_global_device_ids=true, to_apply=%add.19 | all-reduce | flops 2048 | bytes 8192
  105.1 39.6 %all-gather.1 = bf16[32,96,4]{1,2,0:T(4,128)(2,1)S(1)} all-gather(bf16[1,96,4]{1,2,0:T(4,128)(2,1)S(1)} %bitcast.579), channel_id=1, replica_groups=mesh['fsdp'=32] {'fsdp'}, dimensions={0}, use_global_device_ids=true | all-gather | bytes 25344 | tf_op jit(solution)/shard_map/all_gather | solution.py:198
  146.9 5.7 fusion.206
  152.7 8.4 fusion.153
  192.2 346.2 %while.41 = (s32[]{:T(128)}, f32[6,128,256]{2,1,0:T(8,128)S(1)}, f32[8,64,6,256]{3,1,2,0:T(8,128)}, f32[8,6,128,256]{3,2,1,0:T(8,128)}, f32[8,64,6]{2,1,0:T(8,12...) while((s32[]{:T(128)}, f32[6,128,256]{2,1,0:T(8,128)S(1)}, ...), condition=%wide.region_8.10_spmd.clone, body=%wide.region_6.9_spmd.clone.sunk | while | flops 380199296 | bytes 10105705 | solution.py:108
  199.8 29.5 %custom-call.25 = f32[6,1,64,64]{2,3,1,0:T(8,128)S(1)} custom-call(f32[6,1,64,64]{3,2,1,0:T(8,128)S(1)} %fusion.366), custom_call_target="InvertDiagBlocksLowerTriangular" | custom-call | tf_op jit(solution)/shard_map/jvp()/while/body/eval_jaxpr/jit(_solve_triangular)/vmap()/triangular_solve/custom-call.1 | solution.py:86
  241.6 29.5 %custom-call.25 = f32[6,1,64,64]{2,3,1,0:T(8,128)S(1)} custom-call(f32[6,1,64,64]{3,2,1,0:T(8,128)S(1)} %fusion.366), custom_call_target="InvertDiagBlocksLowerTriangular" | custom-call | tf_op jit(solution)/shard_map/jvp()/while/body/eval_jaxpr/jit(_solve_triangular)/vmap()/triangular_solve/custom-call.1 | solution.py:86
  283.5 29.5 %custom-call.25 = f32[6,1,64,64]{2,3,1,0:T(8,128)S(1)} custom-call(f32[6,1,64,64]{3,2,1,0:T(8,128)S(1)} %fusion.366), custom_call_target="InvertDiagBlocksLowerTriangular" | custom-call | tf_op jit(solution)/shard_map/jvp()/while/body/eval_jaxpr/jit(_solve_triangular)/vmap()/triangular_solve/custom-call.1 | solution.py:86
  325.5 29.5 %custom-call.25 = f32[6,1,64,64]{2,3,1,0:T(8,128)S(1)} custom-call(f32[6,1,64,64]{3,2,1,0:T(8,128)S(1)} %fusion.366), custom_call_target="InvertDiagBlocksLowerTriangular" | custom-call | tf_op jit(solution)/shard_map/jvp()/while/body/eval_jaxpr/jit(_solve_triangular)/vmap()/triangular_solve/custom-call.1 | solution.py:86
  367.3 29.5 %custom-call.25 = f32[6,1,64,64]{2,3,1,0:T(8,128)S(1)} custom-call(f32[6,1,64,64]{3,2,1,0:T(8,128)S(1)} %fusion.366), custom_call_target="InvertDiagBlocksLowerTriangular" | custom-call | tf_op jit(solution)/shard_map/jvp()/while/body/eval_jaxpr/jit(_solve_triangular)/vmap()/triangular_solve/custom-call.1 | solution.py:86
  409.1 29.5 %custom-call.25 = f32[6,1,64,64]{2,3,1,0:T(8,128)S(1)} custom-call(f32[6,1,64,64]{3,2,1,0:T(8,128)S(1)} %fusion.366), custom_call_target="InvertDiagBlocksLowerTriangular" | custom-call | tf_op jit(solution)/shard_map/jvp()/while/body/eval_jaxpr/jit(_solve_triangular)/vmap()/triangular_solve/custom-call.1 | solution.py:86
  451.0 29.5 %custom-call.25 = f32[6,1,64,64]{2,3,1,0:T(8,128)S(1)} custom-call(f32[6,1,64,64]{3,2,1,0:T(8,128)S(1)} %fusion.366), custom_call_target="InvertDiagBlocksLowerTriangular" | custom-call | tf_op jit(solution)/shard_map/jvp()/while/body/eval_jaxpr/jit(_solve_triangular)/vmap()/triangular_solve/custom-call.1 | solution.py:86
  492.8 29.5 %custom-call.25 = f32[6,1,64,64]{2,3,1,0:T(8,128)S(1)} custom-call(f32[6,1,64,64]{3,2,1,0:T(8,128)S(1)} %fusion.366), custom_call_target="InvertDiagBlocksLowerTriangular" | custom-call | tf_op jit(solution)/shard_map/jvp()/while/body/eval_jaxpr/jit(_solve_triangular)/vmap()/triangular_solve/custom-call.1 | solution.py:86
  538.5 5.8 copy.475
  545.0 5.4 copy.569
  556.0 8.5 multiply_convert_fusion.2
  571.5 8.6 fusion.221
  580.1 8.7 fusion.222
  588.8 11.4 multiply_convert_fusion
  600.2 7.7 fusion.223
  607.9 5.4 multiply_reduce_fusion.11
  622.5 7.7 fusion.160
  635.2 6.6 multiply_reduce_fusion.8
  643.7 5.6 add_add_fusion
  652.0 6.0 fusion.175
  664.2 11.5 pad_maximum_fusion
  681.2 440.3 %while.42 = (s32[]{:T(128)}, f32[6,128,256]{2,1,0:T(8,128)}, f32[8,64,6,128]{3,1,2,0:T(8,128)}, f32[8,64,6,128]{3,1,2,0:T(8,128)}, f32[8,64,6,256]{3,1,2,0:T(8,1...) while((s32[]{:T(128)}, f32[6,128,256]{2,1,0:T(8,128)}, ...), condition=%wide.region_24.26_spmd.clone, body=%wide.region_13.25_spmd.clone.sunk | while | flops 1044111488 | bytes 35739396 | solution.py:108
  690.5 30.9 %custom-call.26 = f32[6,1,64,64]{2,3,1,0:T(8,128)} custom-call(f32[6,1,64,64]{3,2,1,0:T(8,128)} %select_bitcast_fusion.5), custom_call_target="InvertDiagBlocksLowerTriangular" | custom-call | tf_op jit(solution)/shard_map/transpose(jvp())/while/body/eval_jaxpr/checkpoint/jit(_solve_triangular)/vmap()/triangular_solve | solution.py:86
  745.7 30.9 %custom-call.26 = f32[6,1,64,64]{2,3,1,0:T(8,128)} custom-call(f32[6,1,64,64]{3,2,1,0:T(8,128)} %select_bitcast_fusion.5), custom_call_target="InvertDiagBlocksLowerTriangular" | custom-call | tf_op jit(solution)/shard_map/transpose(jvp())/while/body/eval_jaxpr/checkpoint/jit(_solve_triangular)/vmap()/triangular_solve | solution.py:86
  800.9 30.9 %custom-call.26 = f32[6,1,64,64]{2,3,1,0:T(8,128)} custom-call(f32[6,1,64,64]{3,2,1,0:T(8,128)} %select_bitcast_fusion.5), custom_call_target="InvertDiagBlocksLowerTriangular" | custom-call | tf_op jit(solution)/shard_map/transpose(jvp())/while/body/eval_jaxpr/checkpoint/jit(_solve_triangular)/vmap()/triangular_solve | solution.py:86
  856.1 30.9 %custom-call.26 = f32[6,1,64,64]{2,3,1,0:T(8,128)} custom-call(f32[6,1,64,64]{3,2,1,0:T(8,128)} %select_bitcast_fusion.5), custom_call_target="InvertDiagBlocksLowerTriangular" | custom-call | tf_op jit(solution)/shard_map/transpose(jvp())/while/body/eval_jaxpr/checkpoint/jit(_solve_triangular)/vmap()/triangular_solve | solution.py:86
  911.3 30.9 %custom-call.26 = f32[6,1,64,64]{2,3,1,0:T(8,128)} custom-call(f32[6,1,64,64]{3,2,1,0:T(8,128)} %select_bitcast_fusion.5), custom_call_target="InvertDiagBlocksLowerTriangular" | custom-call | tf_op jit(solution)/shard_map/transpose(jvp())/while/body/eval_jaxpr/checkpoint/jit(_solve_triangular)/vmap()/triangular_solve | solution.py:86
  966.4 30.9 %custom-call.26 = f32[6,1,64,64]{2,3,1,0:T(8,128)} custom-call(f32[6,1,64,64]{3,2,1,0:T(8,128)} %select_bitcast_fusion.5), custom_call_target="InvertDiagBlocksLowerTriangular" | custom-call | tf_op jit(solution)/shard_map/transpose(jvp())/while/body/eval_jaxpr/checkpoint/jit(_solve_triangular)/vmap()/triangular_solve | solution.py:86
  1021.6 30.9 %custom-call.26 = f32[6,1,64,64]{2,3,1,0:T(8,128)} custom-call(f32[6,1,64,64]{3,2,1,0:T(8,128)} %select_bitcast_fusion.5), custom_call_target="InvertDiagBlocksLowerTriangular" | custom-call | tf_op jit(solution)/shard_map/transpose(jvp())/while/body/eval_jaxpr/checkpoint/jit(_solve_triangular)/vmap()/triangular_solve | solution.py:86
  1076.7 30.9 %custom-call.26 = f32[6,1,64,64]{2,3,1,0:T(8,128)} custom-call(f32[6,1,64,64]{3,2,1,0:T(8,128)} %select_bitcast_fusion.5), custom_call_target="InvertDiagBlocksLowerTriangular" | custom-call | tf_op jit(solution)/shard_map/transpose(jvp())/while/body/eval_jaxpr/checkpoint/jit(_solve_triangular)/vmap()/triangular_solve | solution.py:86
  1153.3 5.7 fusion.225
  1159.1 5.5 add_add_fusion.4
  1164.7 10.4 multiply_reduce_fusion.7
  1186.6 6.7 fusion.224
  1197.6 6.1 fusion.199
  1203.7 6.2 fusion.226
  1209.9 5.9 fusion.227
  1215.8 6.5 fusion.202
  1222.3 50.0 %concatenate.18 = f32[1024,10254]{1,0:T(8,128)} concatenate(f32[1024,1]{1,0:T(8,128)S(1)} %copy.503, f32[1024,3072]{1,0:T(8,128)} %fusion.202, f32[1024,12]{1,0:T(8,128)S(1)} %copy-done.32, f32[1024,1536]{1,0:T(8,128)} %fusion.199, f32[1024,1]{1,0:T(8,128)S(1)} %copy.505, f32[1024,2816]{1,0:T(8,128)} %fusion.226, f32[1024,2816]{1,0:T(8,128)} %fusion.227), dimensions={1} | concatenate | bytes 84000768 | tf_op jit(solution)/shard_map/concatenate | solution.py:142
  1273.0 37.5 %all-reduce.21 = (f32[3072,4]{0,1:T(4,128)S(1)}, f32[2,6]{1,0:T(2,128)}, f32[256]{0:T(256)}) all-reduce(f32[3072,4]{0,1:T(4,128)S(1)} %pad_add_fusion, f32[2,6]{1,0:T(2,128)S(1)} %pad_add_fusion.1, f32[256]{0:T(256)S(1)} %copy-done.69), channel_id=1, replica_groups=mesh['fsdp'=32] {'fsdp'}, use_global_device_ids=true, to_apply=%region_35.37 | all-reduce | flops 12556 | bytes 100448 | tf_op jit(solution)/shard_map/psum | solution.py:300
  1316.3 7.7 multiply_convert_fusion.3
  1327.4 320.2 %reduce-scatter.3.cloned.1.call-done = f32[32,10254]{1,0:T(8,128)} async-done(((f32[1024,10254]{1,0:T(8,128)}), f32[32,10254]{1,0:T(8,128)}) %reduce-scatter.3.cloned.1.call-update) | async-done | bytes 1312528 | tf_op jit(solution)/shard_map/reduce_scatter | solution.py:307
  (940 shorter events, 437.1 us)
Async XLA Ops:
  7.2 139.7 %copy-start.15 = (bf16[512,1024]{1,0:T(8,128)(2,1)S(1)}, bf16[512,1024]{1,0:T(8,128)(2,1)}, u32[]{:S(2)}) copy-start(bf16[512,1024]{1,0:T(8,128)(2,1)} %param.21) | copy-start | bytes 3145732
  7.2 97.9 %copy-start.70 = (bf16[96,4]{0,1:T(4,128)(2,1)S(1)}, bf16[96,4]{0,1:T(4,128)(2,1)}, u32[]{:S(2)}) copy-start(bf16[96,4]{0,1:T(4,128)(2,1)} %param.25) | copy-start | bytes 2308
  7.2 139.7 %all-gather.9.cloned.1.call-start = ((), (), s32[]{:S(2)}) async-start(), calls=%async_computation.2 | async-start | bytes 6488064 | tf_op jit(solution)/shard_map/all_gather | solution.py:197
  7.9 548.0 %all-gather.11.cloned.1.call-start = ((), (), s32[]{:S(2)}) async-start(), calls=%async_computation.3 | async-start | bytes 3244032 | tf_op jit(solution)/shard_map/all_gather | solution.py:200
  8.7 555.8 %all-gather.13.cloned.1.call-start = ((), (), s32[]{:S(2)}) async-start(), calls=%async_computation.4 | async-start | bytes 3244032 | tf_op jit(solution)/shard_map/all_gather | solution.py:201
  9.4 562.1 %all-gather.15.cloned.1.call-start = ((), (), s32[]{:S(2)}) async-start(), calls=%async_computation.5 | async-start | bytes 5947392 | tf_op jit(solution)/shard_map/all_gather | solution.py:203
  10.0 570.1 %all-gather.17.cloned.1.call-start = ((), (), s32[]{:S(2)}) async-start(), calls=%async_computation.6 | async-start | bytes 5947392 | tf_op jit(solution)/shard_map/all_gather | solution.py:204
  10.6 578.2 %all-gather.19.cloned.1.call-start = ((), (), s32[]{:S(2)}) async-start(), calls=%async_computation.7 | async-start | bytes 5947392 | tf_op jit(solution)/shard_map/all_gather | solution.py:205
  11.2 1312.8 %reduce-scatter.5.cloned.1.call-start = ((), (), s32[]{:S(2)}) async-start(), calls=%async_computation.9 | async-start | bytes 18382848 | tf_op jit(solution)/shard_map/reduce_scatter | solution.py:310
  13.6 139.1 %copy-start.62 = (pred[512]{0:T(512)(128)(4,1)}, pred[512]{0:T(512)(128)(4,1)S(1)}, u32[]{:S(2)}) copy-start(pred[512]{0:T(512)(128)(4,1)S(1)} %get-tuple-element.953) | copy-start | bytes 1540
  13.6 139.1 %copy-start.64 = (pred[512]{0:T(512)(128)(4,1)}, pred[512]{0:T(512)(128)(4,1)S(1)}, u32[]{:S(2)}) copy-start(pred[512]{0:T(512)(128)(4,1)S(1)} %get-tuple-element.954) | copy-start | bytes 1540
  13.6 139.1 %copy-start.66 = (pred[512]{0:T(512)(128)(4,1)}, pred[512]{0:T(512)(128)(4,1)S(1)}, u32[]{:S(2)}) copy-start(pred[512]{0:T(512)(128)(4,1)S(1)} %get-tuple-element.955) | copy-start | bytes 1540
  59.5 85.2 %copy-start.39 = (bf16[1024,12]{0,1:T(8,128)(2,1)}, bf16[1024,12]{0,1:T(8,128)(2,1)S(1)}, u32[]{:S(2)}) copy-start(bf16[1024,12]{0,1:T(8,128)(2,1)S(1)} %reshape.489) | copy-start | bytes 73732
  99.5 456.5 %copy-start.51 = (f32[1024]{0:T(1024)}, f32[1024]{0:T(1024)S(1)}, u32[]{:S(2)}) copy-start(f32[1024]{0:T(1024)S(1)} %convert_element_type.104) | copy-start | bytes 12292
  101.6 454.4 %copy-start.55 = (f32[512]{0:T(512)}, f32[512]{0:T(512)S(1)}, u32[]{:S(2)}) copy-start(f32[512]{0:T(512)S(1)} %fusion.194) | copy-start | bytes 6148
  144.9 7.8 copy-start.43
  144.9 7.8 copy-start.45
  144.9 7.8 copy-start.47
  144.9 7.8 copy-start.49
  152.6 8.5 copy-start
  538.4 5.8 copy-start.2
  600.1 7.8 copy-start.80
  600.1 7.8 copy-start.78
  600.2 7.8 copy-start.18
  600.2 7.8 copy-start.75
  622.5 7.7 copy-start.9
  675.7 971.9 %reduce-scatter.3.cloned.1.call-start = ((), (), s32[]{:S(2)}) async-start(), calls=%async_computation.8 | async-start | bytes 43794432 | tf_op jit(solution)/shard_map/reduce_scatter | solution.py:307
  1149.7 9.4 slice-start.2
  1153.3 5.8 slice-start.3
  1153.3 5.8 copy-start.20
  1153.3 5.8 copy-start.21
  1153.3 5.8 copy-start.22
  1159.0 5.6 slice-start
  1164.6 10.5 copy-start.50
  1164.6 10.5 copy-start.74
  1186.5 6.8 copy-start.26
  1186.5 6.8 copy-start.16
  1186.5 6.8 copy-start.28
  1186.5 6.8 copy-start.40
  1186.6 6.8 copy-start.52
  1186.6 6.8 copy-start.56
  1197.6 6.1 copy-start.30
  1197.6 6.1 copy-start.81
  1203.7 6.2 copy-start.79
  1209.9 5.9 copy-start.27
  1215.7 6.5 copy-start.32
  1272.3 38.9 %copy-start.54 = (f32[512]{0:T(512)S(1)}, f32[512]{0:T(512)}, u32[]{:S(2)}) copy-start(f32[512]{0:T(512)} %copy-done.53) | copy-start | bytes 6148
  1272.3 38.9 %copy-start.11 = (f32[512,1024]{1,0:T(8,128)S(1)}, f32[512,1024]{1,0:T(8,128)}, u32[]{:S(2)}) copy-start(f32[512,1024]{1,0:T(8,128)} %copy-done.9) | copy-start | bytes 6291460
  (60 other events, 188.8 us)
Sparse Core Ops, SparseCore 0:
  10.9 73.3 all-gather.8
  87.2 57.6 all-gather.10
  147.7 57.9 all-gather.12
  208.4 68.2 all-gather.14
  279.4 67.1 all-gather.16
  349.2 66.8 all-gather.18
  675.8 189.5 reduce-scatter.4
  1272.4 375.1 reduce-scatter.2
where the time goes:
time: 1670 us; the launch traced here: 1660 us
  other arithmetic  597 us (36%)
  waiting for transfers between devices  324 us (19%)
  matrix products  311 us (19%)
  local copies, waits for them, and re-layouts  232 us (14%)
  blocking collectives  160 us (10%)
  loops' own time  24.4 us (1%)
    another operation x40, other arithmetic, group_step(): jax.scipy.linalg.solve_triangular(identity + coupling, target, lower=True)  490 us
    reduce_scatter x1, waiting for transfers between devices, shards(): lax.psum_scatter(wide_joined, 'fsdp', scatter_dimension=0, tiled=True)  320 us
    concatenate x1, local copies, waits for them, and re-layouts, side_by_side(): jnp.concatenate([member if member.ndim == 2 else member[:, None] for memb...  50 us
    all_gather x1, blocking collectives, shards(): lax.all_gather(rate_proj, 'fsdp', axis=0, tiled=True)  44.3 us
    squeeze x40, local copies, waits for them, and re-layouts, delta_rule(): lax.scan(jax.checkpoint(group_step), initial, (to_blocks(queries), to_blo...  39.8 us
    all_gather x1, blocking collectives, shards(): lax.all_gather(conv_taps, 'fsdp', axis=0, tiled=True)  39.6 us
    unnamed x1, blocking collectives  38.2 us
    psum x1, blocking collectives, shards(): small_sums = lax.psum((grad_dparams, grad_hgain, grad_taps), 'fsdp')  37.5 us
  transfers between devices with their start and end apart: 8, of which 1 were waited for; matrix products, arithmetic and copies ran while one was open for 62% of the time, Pallas kernels for 0%

commit v1 on v0

v1 whole, which is shorter than its diff:
```python
import jax
import jax.numpy as jnp
from jax import lax
from jax.experimental import pallas as pl
from jax.experimental.pallas import tpu as pltpu
from jax.sharding import PartitionSpec as P

NH = 6
DK = 128
DV = 256
CONV = 4
GROUP = 64
PIECE = 512


EPS = 1e-06


def rms_norm(values, norm_gain):
    return values * lax.rsqrt(jnp.mean(values * values, axis=-1, keepdims=True) + EPS) * norm_gain


def layout(lengths, row_count):
    padded = (lengths + GROUP - 1) // GROUP * GROUP
    starts = jnp.cumsum(padded) - padded
    offset = jnp.arange(row_count, dtype=jnp.int32)[:, None] - starts[None, :]
    inside = (offset >= 0) & (offset < padded[None, :])
    live_rows = jnp.sum(jnp.where(inside & (offset < lengths[None, :]), 1.0, 0.0), axis=1).astype(
        jnp.float32
    )
    position = jnp.sum(jnp.where(inside, offset, 0), axis=1)
    return (live_rows, position)


def short_conv(mixed_rows, tap_values, position):
    summed = mixed_rows * tap_values[:, CONV - 1]
    for distance in range(1, CONV):
        shifted = jnp.concatenate(
            [jnp.zeros((distance, mixed_rows.shape[1]), mixed_rows.dtype), mixed_rows[:-distance]],
            axis=0,
        )
        summed = (
            summed
            + jnp.where((position >= distance)[:, None], shifted, 0.0)
            * tap_values[:, CONV - 1 - distance]
        )
    return summed


def qkv_heads(mixed_rows, tap_values, position):
    row_count = mixed_rows.shape[0]
    activated = jax.nn.silu(short_conv(mixed_rows, tap_values, position))
    queries = activated[:, : NH * DK].reshape(row_count, NH, DK)
    keys = activated[:, NH * DK : 2 * NH * DK].reshape(row_count, NH, DK)
    values = activated[:, 2 * NH * DK :].reshape(row_count, NH, DV)
    queries = (
        queries * lax.rsqrt(jnp.sum(queries * queries, axis=-1, keepdims=True) + EPS) * DK ** (-0.5)
    )
    keys = keys * lax.rsqrt(jnp.sum(keys * keys, axis=-1, keepdims=True) + EPS)
    return (queries, keys, values)


def gates(rate_logits, decay_params, live_rows):
    write_rate = jax.nn.sigmoid(rate_logits[:, :NH]) * live_rows[:, None]
    log_decay = (
        -jnp.exp(decay_params[0])
        * jax.nn.softplus(rate_logits[:, NH:] + decay_params[1])
        * live_rows[:, None]
    )
    return (write_rate, log_decay)


ROWS_COLS = (((1,), (0,)), ((), ()))
COLS_COLS = (((1,), (1,)), ((), ()))
ROWS_ROWS = (((0,), (0,)), ((), ()))


def product(left, right, dims=ROWS_COLS):
    return lax.dot_general(
        left.astype(jnp.bfloat16),
        right.astype(jnp.bfloat16),
        dims,
        preferred_element_type=jnp.float32,
    )


def halves(values):
    high = values.astype(jnp.bfloat16)
    return (high, (values - high.astype(jnp.float32)).astype(jnp.bfloat16))


def right_split(left, right, dims=ROWS_COLS):
    high, rest = halves(right)
    return product(left, high, dims) + product(left, rest, dims)


def left_split(left, right, dims=ROWS_COLS):
    high, rest = halves(left)
    return product(high, right, dims) + product(rest, right, dims)


def triple(left, right, dims=ROWS_COLS):
    left_high, left_rest = halves(left)
    right_high, right_rest = halves(right)
    return (
        product(left_high, right_high, dims)
        + product(left_high, right_rest, dims)
        + product(left_rest, right_high, dims)
    )


def head_slice(ref, head, width):
    return ref[:, head * width : (head + 1) * width]


def triangle():
    row = lax.broadcasted_iota(jnp.int32, (GROUP, GROUP), 0)
    column = lax.broadcasted_iota(jnp.int32, (GROUP, GROUP), 1)
    return (row, column)


def core_forward_kernel(
    restart_ref, q_ref, k_ref, v_ref, scal_ref, decay_ref, out_ref, start_ref, inv_ref, pseudo_ref, state
):
    step = pl.program_id(0)

    @pl.when(step == 0)
    def _():
        state[...] = jnp.zeros_like(state)

    keep = 1.0 - restart_ref[step]
    row, column = triangle()
    lower = row >= column
    strict = row > column
    identity = jnp.where(row == column, 1.0, 0.0)
    withins = []
    couplings = []
    query_keys = []
    inverses = []
    heads = range(NH)
    for head in heads:
        queries = head_slice(q_ref, head, DK)
        keys = head_slice(k_ref, head, DK)
        write = scal_ref[:, head : head + 1]
        decay = scal_ref[:, NH + head : NH + head + 1]
        gaps = decay - decay_ref[0, head : head + 1, :]
        within = jnp.where(lower, jnp.exp(jnp.where(lower, gaps, 0.0)), 0.0)
        both = product(jnp.concatenate([keys, queries], axis=0), keys, COLS_COLS)
        coupling = jnp.where(strict, write * within * both[:GROUP], 0.0)
        couplings.append(coupling)
        query_keys.append(both[GROUP:] * within)
        pair = (row == column + 1) & (row % 2 == 1)
        inverses.append(identity - jnp.where(pair, coupling, 0.0))
    size = 2
    while size < GROUP:
        below = (row // size) % 2 == 1
        pair = below & (row // size == column // size + 1)
        firsts = [triple(inverses[head], jnp.where(pair, couplings[head], 0.0)) for head in heads]
        inverses = [inverses[head] - triple(firsts[head], inverses[head]) for head in heads]
        size = size * 2
    for head in heads:
        queries = head_slice(q_ref, head, DK)
        keys = head_slice(k_ref, head, DK)
        values = head_slice(v_ref, head, DV).astype(jnp.float32)
        write = scal_ref[:, head : head + 1]
        decay = scal_ref[:, NH + head : NH + head + 1]
        grown = jnp.exp(decay)
        start = state[head] * keep
        start_ref[0, head] = start
        inv_ref[0, head] = inverses[head]
        both = right_split(jnp.concatenate([keys, queries], axis=0), start)
        target = write * values - write * grown * both[:GROUP]
        pseudo = triple(inverses[head], target)
        pseudo_ref[:, head * DV : (head + 1) * DV] = pseudo
        out_ref[:, head * DV : (head + 1) * DV] = grown * both[GROUP:] + triple(
            query_keys[head], pseudo
        )
        last = decay[GROUP - 1 :, :]
        tail = jnp.exp(last - decay)
        state[head] = jnp.exp(last) * start + right_split(keys, tail * pseudo, ROWS_ROWS)


def core_backward_kernel(
    restart_ref,
    q_ref,
    k_ref,
    v_ref,
    scal_ref,
    decay_ref,
    start_ref,
    inv_ref,
    pseudo_ref,
    dout_ref,
    dq_ref,
    dk_ref,
    dv_ref,
    dscal_ref,
    ddecay_ref,
    costate,
):
    step = pl.program_id(0)

    @pl.when(step == 0)
    def _():
        costate[...] = jnp.zeros_like(costate)

    keep = 1.0 - restart_ref[pl.num_programs(0) - 1 - step]
    row, column = triangle()
    lower = row >= column
    strict = row > column
    final = lax.broadcasted_iota(jnp.int32, (GROUP, 1), 0) == GROUP - 1
    ddecay_ref[...] = jnp.zeros_like(ddecay_ref)
    for head in range(NH):
        queries = head_slice(q_ref, head, DK)
        keys = head_slice(k_ref, head, DK)
        values = head_slice(v_ref, head, DV).astype(jnp.float32)
        wide_keys = keys.astype(jnp.float32)
        wide_queries = queries.astype(jnp.float32)
        write = scal_ref[:, head : head + 1]
        decay = scal_ref[:, NH + head : NH + head + 1]
        start = start_ref[0, head]
        pseudo = head_slice(pseudo_ref, head, DV)
        dout = head_slice(dout_ref, head, DV)
        dstate = costate[head]
        gaps = decay - decay_ref[0, head : head + 1, :]
        within = jnp.where(lower, jnp.exp(jnp.where(lower, gaps, 0.0)), 0.0)
        keys_queries = jnp.concatenate([keys, queries], axis=0)
        both = product(keys_queries, keys, COLS_COLS)
        key_key = jnp.where(strict, both[:GROUP] * within, 0.0)
        query_key = both[GROUP:] * within
        grown = jnp.exp(decay)
        last = decay[GROUP - 1 :, :]
        tail = jnp.exp(last - decay)
        dpseudo = triple(query_key, dout, ROWS_ROWS) + tail * right_split(keys, dstate)
        dtarget = triple(inv_ref[0, head], dpseudo, ROWS_ROWS)
        stacked = jnp.concatenate([dtarget, dout], axis=0)
        pairs = triple(stacked, pseudo, COLS_COLS)
        dcoupling = jnp.where(strict, -pairs[:GROUP], 0.0)
        dquery_key = jnp.where(lower, pairs[GROUP:], 0.0)
        reads = triple(stacked, start, COLS_COLS)
        dread_key = reads[:GROUP]
        dq_state = grown * reads[GROUP:]
        inner = dquery_key * within
        dkey_key = dcoupling * write * within
        dq_ref[:, head * DK : (head + 1) * DK] = dq_state + left_split(inner, keys)
        scaled = write * grown
        dtail = tail * triple(pseudo, dstate, COLS_COLS)
        dk_ref[:, head * DK : (head + 1) * DK] = (
            left_split(jnp.concatenate([dkey_key, inner], axis=0), keys_queries, ROWS_ROWS)
            + left_split(dkey_key, keys)
            - scaled * dread_key
            + dtail
        )
        dv_ref[:, head * DV : (head + 1) * DV] = write * dtarget
        read_key = jnp.sum(dread_key * wide_keys, axis=1, keepdims=True)
        dscal_ref[:, head : head + 1] = (
            jnp.sum(dtarget * values, axis=1, keepdims=True)
            - grown * read_key
            + jnp.sum(dcoupling * key_key, axis=1, keepdims=True)
        )
        weight = dquery_key * query_key + dcoupling * write * key_key
        moved = jnp.sum(dtail * wide_keys, axis=1, keepdims=True)
        at_last = jnp.sum(moved, axis=0, keepdims=True) + jnp.exp(last) * jnp.sum(
            jnp.sum(start * dstate, axis=1, keepdims=True), axis=0, keepdims=True
        )
        dscal_ref[:, NH + head : NH + head + 1] = (
            jnp.sum(dq_state * wide_queries, axis=1, keepdims=True)
            - scaled * read_key
            + jnp.sum(weight, axis=1, keepdims=True)
            - moved
            + jnp.where(final, at_last, 0.0)
        )
        ddecay_ref[0, head : head + 1, :] = -jnp.sum(weight, axis=0, keepdims=True)
        sources = jnp.concatenate([-scaled * dtarget, grown * dout], axis=0)
        costate[head] = keep * (
            jnp.exp(last) * dstate + right_split(keys_queries, sources, ROWS_ROWS)
        )


def core_specs(blocks, backward):
    def at(step):
        return blocks - 1 - step if backward else step

    def rows(width):
        return pl.BlockSpec((GROUP, width), lambda step: (at(step), 0))

    def lead(*shape):
        return pl.BlockSpec((1,) + shape, lambda step: (at(step),) + (0,) * len(shape))

    return rows, lead


def core_forward(restart, queries, keys, values, scalars, decay_rows):
    row_count = queries.shape[0]
    blocks = row_count // GROUP
    rows, lead = core_specs(blocks, False)
    wide = jax.ShapeDtypeStruct((row_count, NH * DV), jnp.float32)
    return pl.pallas_call(
        core_forward_kernel,
        grid=(blocks,),
        in_specs=[
            pl.BlockSpec(memory_space=pltpu.SMEM),
            rows(NH * DK),
            rows(NH * DK),
            rows(NH * DV),
            rows(2 * NH),
            lead(8, GROUP),
        ],
        out_specs=[rows(NH * DV), lead(NH, DK, DV), lead(NH, GROUP, GROUP), rows(NH * DV)],
        out_shape=[
            wide,
            jax.ShapeDtypeStruct((blocks, NH, DK, DV), jnp.float32),
            jax.ShapeDtypeStruct((blocks, NH, GROUP, GROUP), jnp.float32),
            wide,
        ],
        scratch_shapes=[pltpu.VMEM((NH, DK, DV), jnp.float32)],
        compiler_params=pltpu.CompilerParams(vmem_limit_bytes=24 * 2**20),
        cost_estimate=pl.CostEstimate(
            flops=40_000_000_000, bytes_accessed=20_000_000, transcendentals=400_000
        ),
    )(restart, queries, keys, values, scalars, decay_rows)


def core_backward(restart, queries, keys, values, scalars, decay_rows, kept, d_recurrent):
    row_count = queries.shape[0]
    blocks = row_count // GROUP
    rows, lead = core_specs(blocks, True)
    narrow = jax.ShapeDtypeStruct((row_count, NH * DK), jnp.float32)
    return pl.pallas_call(
        core_backward_kernel,
        grid=(blocks,),
        in_specs=[
            pl.BlockSpec(memory_space=pltpu.SMEM),
            rows(NH * DK),
            rows(NH * DK),
            rows(NH * DV),
            rows(2 * NH),
            lead(8, GROUP),
            lead(NH, DK, DV),
            lead(NH, GROUP, GROUP),
            rows(NH * DV),
            rows(NH * DV),
        ],
        out_specs=[
            rows(NH * DK),
            rows(NH * DK),
            rows(NH * DV),
            rows(2 * NH),
            lead(8, GROUP),
        ],
        out_shape=[
            narrow,
            narrow,
            jax.ShapeDtypeStruct((row_count, NH * DV), jnp.float32),
            jax.ShapeDtypeStruct((row_count, 2 * NH), jnp.float32),
            jax.ShapeDtypeStruct((blocks, 8, GROUP), jnp.float32),
        ],
        scratch_shapes=[pltpu.VMEM((NH, DK, DV), jnp.float32)],
        compiler_params=pltpu.CompilerParams(vmem_limit_bytes=24 * 2**20),
        cost_estimate=pl.CostEstimate(
            flops=40_000_000_000, bytes_accessed=20_000_000, transcendentals=400_000
        ),
    )(restart, queries, keys, values, scalars, decay_rows, *kept, d_recurrent)


def core_scalars(rate_logits, decay_params, live_rows):
    write_rate, log_decay = gates(rate_logits, decay_params, live_rows)
    blocks = log_decay.shape[0] // GROUP
    lower = jnp.tril(jnp.ones((GROUP, GROUP), jnp.float32))
    total = jnp.einsum(
        "ti,cih->cth",
        lower,
        log_decay.reshape(blocks, GROUP, NH),
        precision=lax.Precision.HIGHEST,
    )
    decay_rows = jnp.pad(total.transpose(0, 2, 1), ((0, 0), (0, 8 - NH), (0, 0)))
    return (jnp.concatenate([write_rate, total.reshape(-1, NH)], axis=1), decay_rows)


def gated_norm(recurrent, gate_logits, head_gain):
    row_count = recurrent.shape[0]
    return rms_norm(recurrent, head_gain) * jax.nn.silu(gate_logits.reshape(row_count, NH, DV))


def swiglu(gate_in, up_in):
    return jax.nn.silu(gate_in) * up_in


def by_owner(members, owners):
    return jnp.concatenate(
        [
            member[:, first : first + PIECE].reshape(owners, -1, PIECE)
            for member in members
            for first in range(0, member.shape[1], PIECE)
        ],
        axis=1,
    ).reshape(-1, PIECE)


def from_owner(joined, shapes):
    members = []
    first = 0
    for height, width in shapes:
        columns = []
        for _ in range(width // PIECE):
            columns.append(joined[first : first + height])
            first = first + height
        members.append(jnp.concatenate(columns, axis=1))
    return members


def shards(
    inputs,
    seq_lens,
    mixer_gain,
    input_proj,
    conv_taps,
    rate_proj,
    decay_params,
    outgate_proj,
    head_gain,
    output_proj,
    feed_gain,
    gate_proj,
    up_proj,
    down_proj,
    cotangent,
):
    row_count, width = inputs.shape
    owners = lax.axis_size("fsdp")
    live_rows, position = layout(seq_lens[0], row_count)
    restart = jnp.where(position.reshape(-1, GROUP)[:, 0] == 0, 1.0, 0.0).astype(jnp.float32)
    my_rows = mixer_gain.shape[0]
    qkv, gate_width, ff = input_proj.shape[1], outgate_proj.shape[1], gate_proj.shape[1]
    tap_flat = conv_taps.size // my_rows
    first_rate = qkv + gate_width
    first_tap = first_rate + 2 * NH
    used = first_tap + tap_flat + 2
    spare = -used % 128
    mixer_packed = jnp.concatenate(
        [
            input_proj,
            outgate_proj,
            rate_proj,
            conv_taps.reshape(my_rows, tap_flat),
            mixer_gain[:, None],
            feed_gain[:, None],
            jnp.zeros((my_rows, spare), jnp.bfloat16),
        ],
        axis=1,
    )
    full_mixer = lax.all_gather(mixer_packed, "fsdp", axis=0, tiled=True)
    feed_packed = jnp.concatenate([gate_proj, up_proj], axis=1)
    tall_packed = jnp.concatenate([output_proj, down_proj], axis=0)
    feed_packed, tall_packed, full_mixer = lax.optimization_barrier(
        (feed_packed, tall_packed, full_mixer)
    )
    full_tall = lax.all_gather(tall_packed, "fsdp", axis=0, tiled=False)
    full_feed = lax.all_gather(feed_packed, "fsdp", axis=0, tiled=True)
    out_rows = output_proj.shape[0]
    full_out = full_tall[:, :out_rows].reshape(-1, width)
    full_down = full_tall[:, out_rows:].reshape(-1, width)
    full_taps = full_mixer[:, first_tap : first_tap + tap_flat].reshape(-1, CONV)
    full_mgain = full_mixer[:, used - 2]
    full_fgain = full_mixer[:, used - 1]
    stream = inputs.astype(jnp.float32)
    normed_wide, norm_one_back = jax.vjp(rms_norm, stream, full_mgain.astype(jnp.float32))
    normed = normed_wide.astype(jnp.bfloat16)
    projected = jnp.dot(normed, full_mixer, preferred_element_type=jnp.float32)
    mixed_in = projected[:, :qkv]
    gate_logits = projected[:, qkv:first_rate]
    rate_logits = projected[:, first_rate:first_tap]

    def heads_fn(mixed_rows, tap_values):
        return qkv_heads(mixed_rows, tap_values, position)

    (queries, keys, values), heads_back = jax.vjp(heads_fn, mixed_in, full_taps.astype(jnp.float32))
    core_inputs = (
        restart,
        queries.reshape(row_count, NH * DK).astype(jnp.bfloat16),
        keys.reshape(row_count, NH * DK).astype(jnp.bfloat16),
        values.reshape(row_count, NH * DV).astype(jnp.bfloat16),
    )

    def scalars_fn(rate_in, param_in):
        return core_scalars(rate_in, param_in, live_rows)

    scalar_values, scalars_back = jax.vjp(scalars_fn, rate_logits, decay_params)
    recurrent_flat, *kept = core_forward(*core_inputs, *scalar_values)
    recurrent = recurrent_flat.reshape(row_count, NH, DV)
    head_normed, head_back = jax.vjp(gated_norm, recurrent, gate_logits, head_gain)
    head_out = head_normed.reshape(row_count, NH * DV).astype(jnp.bfloat16)
    middle = stream + jnp.dot(head_out, full_out, preferred_element_type=jnp.float32)
    normed_two_wide, norm_two_back = jax.vjp(rms_norm, middle, full_fgain.astype(jnp.float32))
    normed_two = normed_two_wide.astype(jnp.bfloat16)
    feed_act = jnp.dot(normed_two, full_feed, preferred_element_type=jnp.float32)
    gate_act = feed_act[:, :ff]
    up_act = feed_act[:, ff:]
    hidden_wide, swiglu_back = jax.vjp(swiglu, gate_act, up_act)
    hidden = hidden_wide.astype(jnp.bfloat16)
    output = (
        (middle + jnp.dot(hidden, full_down, preferred_element_type=jnp.float32))
        * live_rows[:, None]
    ).astype(jnp.bfloat16)
    d_final = cotangent.astype(jnp.float32) * live_rows[:, None]
    d_ffn = d_final.astype(jnp.bfloat16)
    d_hidden = jnp.einsum("rd,fd->rf", d_ffn, full_down, preferred_element_type=jnp.float32)
    d_gate_wide, d_up_wide = swiglu_back(d_hidden)
    d_feed = jnp.concatenate(
        [d_gate_wide.astype(jnp.bfloat16), d_up_wide.astype(jnp.bfloat16)], axis=1
    )
    grad_feed = jnp.einsum(
        "rd,rf->df", normed_two, d_feed, preferred_element_type=jnp.float32
    ).astype(jnp.bfloat16)
    d_normed_two = jnp.einsum("rf,df->rd", d_feed, full_feed, preferred_element_type=jnp.float32)
    d_middle_part, grad_fgain = norm_two_back(d_normed_two)
    d_middle = d_final + d_middle_part
    d_branch = d_middle.astype(jnp.bfloat16)
    grad_down = jnp.einsum("rf,rd->fd", hidden, d_ffn, preferred_element_type=jnp.float32)
    grad_out = jnp.einsum("rv,rd->vd", head_out, d_branch, preferred_element_type=jnp.float32)
    feed_joined = by_owner(
        (grad_feed, grad_out.astype(jnp.bfloat16), grad_down.astype(jnp.bfloat16)), owners
    )
    feed_joined, d_branch = lax.optimization_barrier((feed_joined, d_branch))
    feed_mine = lax.psum_scatter(feed_joined, "fsdp", scatter_dimension=0, tiled=True)
    d_head = jnp.einsum(
        "rd,vd->rv", d_branch, full_out, preferred_element_type=jnp.float32
    ).reshape(row_count, NH, DV)
    d_recurrent, d_gate_logits, grad_hgain = head_back(d_head)
    d_queries, d_keys, d_values, d_scalars, d_decay_rows = core_backward(
        *core_inputs, *scalar_values, kept, d_recurrent.reshape(row_count, NH * DV)
    )
    d_rates, grad_dparams = scalars_back((d_scalars, d_decay_rows))
    d_mixed, grad_taps = heads_back(
        (
            d_queries.reshape(row_count, NH, DK),
            d_keys.reshape(row_count, NH, DK),
            d_values.reshape(row_count, NH, DV),
        )
    )
    d_projected = jnp.concatenate(
        [
            d_mixed.astype(jnp.bfloat16),
            d_gate_logits.astype(jnp.bfloat16),
            d_rates.astype(jnp.bfloat16),
            jnp.zeros((row_count, tap_flat + 2 + spare), jnp.bfloat16),
        ],
        axis=1,
    )
    grad_mixer = jnp.einsum(
        "rd,rc->dc", normed, d_projected, preferred_element_type=jnp.float32
    ).astype(jnp.bfloat16)
    d_normed = jnp.einsum(
        "rc,dc->rd", d_projected, full_mixer, preferred_element_type=jnp.float32
    )
    d_stream, grad_mgain = norm_one_back(d_normed)
    grad_inputs = d_middle + d_stream
    mixer_mine = lax.psum_scatter(
        grad_mixer, "fsdp", scatter_dimension=0, tiled=True
    ).astype(jnp.float32)
    small = jnp.concatenate(
        [grad_taps.T.reshape(-1), grad_mgain, grad_fgain, grad_hgain, grad_dparams.reshape(-1)]
    )
    small_sum = lax.psum(small, "fsdp")
    me = lax.axis_index("fsdp")
    tap_rows = conv_taps.shape[0]
    taps_sum = small_sum[: qkv * CONV].reshape(CONV, qkv)
    gains_sum = small_sum[qkv * CONV : qkv * CONV + 2 * width].reshape(2, width)
    rest_sum = small_sum[qkv * CONV + 2 * width :]
    taps_mine = lax.dynamic_slice_in_dim(taps_sum, me * tap_rows, tap_rows, 1).T
    gains_mine = lax.dynamic_slice_in_dim(gains_sum, me * my_rows, my_rows, 1)
    gate_up_mine, out_mine, down_mine = from_owner(
        feed_mine.astype(jnp.float32),
        ((my_rows, 2 * ff), (out_rows, width), (down_proj.shape[0], width)),
    )
    return (
        output,
        grad_inputs,
        gains_mine[0],
        mixer_mine[:, :qkv],
        taps_mine,
        mixer_mine[:, first_rate:first_tap],
        rest_sum[head_gain.shape[0] :].reshape(2, NH),
        mixer_mine[:, qkv:first_rate],
        rest_sum[: head_gain.shape[0]],
        out_mine,
        gains_mine[1],
        gate_up_mine[:, :ff],
        gate_up_mine[:, ff:],
        down_mine,
    )


def solution(mesh):
    placed = (
        P("fsdp", None),
        P("fsdp", None),
        P("fsdp"),
        P("fsdp", None),
        P("fsdp", None),
        P("fsdp", None),
        P(),
        P("fsdp", None),
        P(),
        P("fsdp", None),
        P("fsdp"),
        P("fsdp", None),
        P("fsdp", None),
        P("fsdp", None),
        P("fsdp", None),
    )
    return jax.shard_map(
        shards,
        mesh=mesh,
        in_specs=placed,
        out_specs=(
            P("fsdp", None),
            P("fsdp", None),
            P("fsdp"),
            P("fsdp", None),
            P("fsdp", None),
            P("fsdp", None),
            P(),
            P("fsdp", None),
            P(),
            P("fsdp", None),
            P("fsdp"),
            P("fsdp", None),
            P("fsdp", None),
            P("fsdp", None),
        ),
        check_vma=False,
    )
```

time: 1670 us -> 913 us (0.55)
  other arithmetic: 597 us -> 100 us
  matrix products: 311 us -> 99.7 us
  blocking collectives: 160 us -> 42.5 us
  waiting for transfers between devices: 324 us -> 420 us
  local copies, waits for them, and re-layouts: 232 us -> 139 us
  Pallas kernels: 0 us -> 87.3 us
  loops' own time: 24.4 us -> 0 us
    another operation x81 -> x1, other arithmetic: 503 us -> 0.18 us  [the longest x40 490 us: group_step(): jax.scipy.linalg.solve_triangular(identity + coupling, target, lower=True)]
    dot_general x201 -> x10, matrix products: 258 us -> 84.4 us  [the longest x1 13.3 us: shards(): jnp.einsum('rf,df->rd', d_feed, full_feed, preferred_element_type=jnp.flo...]
    all_gather x6 -> x3, waiting for transfers between devices: 0.01 us -> 122 us  [the longest x1 82.6 us: shards(): full_mixer = lax.all_gather(mixer_packed, 'fsdp', axis=0, tiled=True)]
    pallas_call x0 -> x2, Pallas kernels: none -> 87.3 us  [the longest x1 52.1 us: core_backward(): pl.pallas_call(core_backward_kernel, grid=(blocks,), in_specs=[pl.BlockSp...]
    all_gather x2 -> x0, blocking collectives: 83.9 us -> none  [the longest x1 44.3 us: shards(): lax.all_gather(rate_proj, 'fsdp', axis=0, tiled=True)]
    squeeze x48 -> x1, local copies, waits for them, and re-layouts: 39.9 us -> 0.52 us  [shards(): gains_mine[1]]
    concatenate x1 -> x5, local copies, waits for them, and re-layouts: 50 us -> 11.4 us  [the longest x1 7.76 us: shards(): jnp.concatenate([d_mixed.astype(jnp.bfloat16), d_gate_logits.astype(jnp.b...]
    unnamed x1 -> x0, blocking collectives: 38.2 us -> none
  transfers between devices with their start and end apart: 8 -> 5, of which waited for: 1 -> 4; matrix products, arithmetic and copies ran while one was open for 62% -> 14% of each run, Pallas kernels for 0% -> 4%
where the time goes in v1:
time: 913 us; the launch traced here: 903 us
  waiting for transfers between devices  420 us (46%)
  local copies, waits for them, and re-layouts  139 us (15%)
  other arithmetic  100 us (11%)
  matrix products  99.7 us (11%)
  Pallas kernels  87.3 us (10%)
  blocking collectives  42.5 us (5%)
  between operations  15.4 us (2%)
    reduce_scatter x1, waiting for transfers between devices, shards(): lax.psum_scatter(feed_joined, 'fsdp', scatter_dimension=0, tiled=True)  214 us
    all_gather x1, waiting for transfers between devices, shards(): full_mixer = lax.all_gather(mixer_packed, 'fsdp', axis=0, tiled=True)  82.6 us
    reduce_scatter x1, waiting for transfers between devices, shards(): lax.psum_scatter(grad_mixer, 'fsdp', scatter_dimension=0, tiled=True)  82.4 us
    pallas_call x1, Pallas kernels, core_backward(): pl.pallas_call(core_backward_kernel, grid=(blocks,), in_specs=[pl.BlockSp...  52.1 us
    unnamed x193, local copies, waits for them, and re-layouts  46.9 us
    psum x1, blocking collectives, shards(): small_sum = lax.psum(small, 'fsdp')  42.5 us
    all_gather x1, waiting for transfers between devices, shards(): full_feed = lax.all_gather(feed_packed, 'fsdp', axis=0, tiled=True)  39.5 us
    pallas_call x1, Pallas kernels, core_forward(): pl.pallas_call(core_forward_kernel, grid=(blocks,), in_specs=[pl.BlockSpe...  35.2 us
  transfers between devices with their start and end apart: 5, of which 4 were waited for; matrix products, arithmetic and copies ran while one was open for 14% of the time, Pallas kernels for 4%

profile of v1, /device:TPU:0, one launch (start us, length us, event | category | flops | bytes accessed | tf_op | source)
XLA Modules:
  0.0 903.4 jit_solution(10359268387876553845)
XLA Ops:
  15.8 82.6 %all-gather.5.cloned.1.call-done = bf16[1024,4736]{1,0:T(8,128)(2,1)} async-done(((bf16[32,4736]{1,0:T(8,128)(2,1)}), bf16[1024,4736]{1,0:T(8,128)(2,1)}) %all-gather.5.cloned.1.call-update) | async-done | bytes 9699344 | tf_op jit(solution)/shard_map/all_gather | solution.py:452
  106.8 8.6 fusion.29
  115.4 3.9 slice.287
  119.3 3.6 slice.285
  122.9 3.4 slice.283
  128.0 2.9 slice_reduce_fusion.3
  131.0 13.3 %fusion.5 = (f32[512,3072]{1,0:T(8,128)S(1)}, f32[512,3072]{1,0:T(8,128)}) fusion(f32[3072]{0:T(1024)S(1)} %get-tuple-element.153, f32[509,3072]{1,0:T(8,128)S(1)} %copy-done.20, pred[512]{0:T(512)(128)(4,1)S(1)} %get-tuple-element.213, f32[3072]{0:T(1024)S(1)} %get-tuple-element.154, f32[510,3072]{1,0:T(8,128)} %slice.285, ...), kind=kLoop, calls=%fused_computation.18 | loop fusion | flops 22020096 | bytes 37725696 | tf_op jit(solution)/shard_map/jvp(jit(silu))/mul | solution.py:52
  149.4 2.4 copy.193
  157.9 2.6 multiply_convert_fusion.5
  160.5 35.2 %shard_map.254 = (f32[512,1536]{1,0:T(8,128)S(1)}, f32[8,6,128,256]{3,2,1,0:T(8,128)S(1)}, f32[8,6,64,64]{3,2,1,0:T(8,128)S(1)}, f32[512,1536]{1,0:T(8,128)S(1)}) custom-call(f32[8]{0:T(128)S(1)} %select_reduce_fusion.2.restart_ref, bf16[512,768]{1,0:T(8,128)(2,1)S(1)} %get-tuple-element.187.q_ref, bf16[512,768]{1,0:T(8,128)(2,1)S(1)} %get-tuple-element.186.k_ref, ...), custom_call_target="tpu_custom_call" | custom-call | flops 40000000000 | bytes 20000000 | tf_op jit(solution)/shard_map/pallas_call | solution.py:298
  195.7 2.7 copy-done.11
  201.3 2.4 copy.202
  203.7 2.3 multiply_reduce_fusion.6
  208.1 3.7 copy.203
  211.8 6.2 fusion.71
  218.0 3.5 copy.204
  223.8 7.0 slice.298
  230.8 3.2 multiply_reduce_fusion.9
  233.9 39.5 %all-gather.7.cloned.1.call-done = bf16[1024,5632]{1,0:T(8,128)(2,1)} async-done(((bf16[32,5632]{1,0:T(8,128)(2,1)}), bf16[1024,5632]{1,0:T(8,128)(2,1)}) %all-gather.7.cloned.1.call-update) | async-done | bytes 11534352 | tf_op jit(solution)/shard_map/all_gather | solution.py:459
  273.4 12.6 %fusion.64 = f32[512,5632]{1,0:T(8,128)} fusion(bf16[1024,5632]{1,0:T(8,128)(2,1)} %all-gather.7.cloned.1.call-done, f32[512,1024]{1,0:T(8,128)} %get-tuple-element.220, f32[1024]{0:T(1024)S(1)} %get-tuple-element.140, f32[512]{0:T(512)S(1)} %fusion.56), kind=kOutput, calls=%fused_computation.205 | convolution fusion | flops 5907152896 | bytes 25171968 | tf_op jit(solution)/shard_map/dot_general | solution.py:496
  286.0 9.9 %fusion.8 = (bf16[512,2816]{1,0:T(8,128)(2,1)S(1)}, bf16[512,2816]{1,0:T(8,128)(2,1)S(1)}, bf16[512,2816]{1,0:T(8,128)(2,1)}) fusion(f32[512,5632]{1,0:T(8,128)} %fusion.64, bf16[2816,1024]{1,0:T(8,128)(2,1)S(1)} %bitcast.132, bf16[512,1024]{1,0:T(8,128)(2,1)S(1)} %copy-done.39, f32[512]{0:T(512)S(1)} %select_reduce_fusion), kind=kOutput, calls=%fused_computation.25 | convolution fusion | flops 2977431552 | bytes 27002880 | tf_op jit(solution)/shard_map/rd,fd->rf/dot_general | solution.py:507
  298.3 9.4 %convolution_convert_fusion = bf16[1024,5632]{1,0:T(8,128)(2,1)} fusion(bf16[512,2816]{1,0:T(8,128)(2,1)S(1)} %get-tuple-element.164, bf16[512,2816]{1,0:T(8,128)(2,1)S(1)} %get-tuple-element.163, f32[512,1024]{1,0:T(8,128)S(1)} %copy-done.32, f32[1024]{0:T(1024)S(1)} %get-tuple-element.140, f32[512]{0:T(512)S(1)} %fusion.56), kind=kOutput, calls=%fused_computation | convolution fusion | flops 5924454400 | bytes 19404800 | tf_op jit(solution)/shard_map/rd,rf->df/dot_general | solution.py:512
  307.7 13.3 %multiply_reduce_fusion.7 = (f32[1024]{0:T(1024)}, f32[512]{0:T(512)S(1)}, f32[512,1024]{1,0:T(8,128)}) fusion(f32[512,1024]{1,0:T(8,128)S(1)} %copy-done.33, f32[512]{0:T(512)S(1)} %fusion.56, f32[1024]{0:T(1024)S(1)} %get-tuple-element.140, bf16[1024,5632]{1,0:T(8,128)(2,1)} %all-gather.7.cloned.1.call-done, bf16[512,2816]{1,0:T(8,128)(2,1)} %copy-done.78, ...), kind=kOutput, calls=%fused_computation.63 | convolution fusion | flops 5920258560 | bytes 21508096 | tf_op jit(solution)/shard_map/rf,df->rd/dot_general | solution.py:515
  321.0 5.5 fusion.70
  334.2 3.6 convolution_convert_fusion.2
  357.1 8.4 multiply_reduce_fusion.4
  365.5 3.1 add_add_fusion
  368.6 3.5 copy.205.dout_ref
  378.6 2.8 copy-done.12
  384.7 52.1 %shard_map.255 = (f32[512,768]{1,0:T(8,128)S(1)}, f32[512,768]{1,0:T(8,128)S(1)}, f32[512,1536]{1,0:T(8,128)S(1)}, f32[512,12]{1,0:T(8,128)S(1)}, f32[8,8,64]{2,1,0:T(8,128)S(1)}) custom-call(f32[8]{0:T(128)S(1)} %select_reduce_fusion.2.restart_ref, bf16[512,768]{1,0:T(8,128)(2,1)S(1)} %copy-done.8, bf16[512,768]{1,0:T(8,128)(2,1)S(1)} %copy-done.6, ...), custom_call_target="tpu_custom_call" | custom-call | flops 40000000000 | bytes 20000000 | tf_op jit(solution)/shard_map/pallas_call | solution.py:329
  438.5 2.9 slice_multiply_fusion.3
  441.4 3.2 copy.207
  447.5 3.1 copy.208
  450.7 5.4 add_add_fusion.4
  462.0 3.0 add_add_fusion.3
  465.8 13.6 %multiply_reduce_fusion.3 = (f32[3072]{0:T(1024)S(1)}, f32[3072]{0:T(1024)S(1)}, f32[3072]{0:T(1024)S(1)}, f32[3072]{0:T(1024)S(1)}, f32[512,3072]{1,0:T(8,128)S(1)}) fusion(f32[509,3072]{1,0:T(8,128)} %slice.287, pred[512]{0:T(512)(128)(4,1)S(1)} %copy-done.67, f32[512,4736]{1,0:T(8,128)} %copy-done.18, f32[511,3072]{1,0:T(8,128)} %slice.283, ...), kind=kLoop, calls=%fused_computation.15 | loop fusion | flops 34590720 | bytes 44017152 | tf_op jit(solution)/shard_map/transpose(jvp())/reduce_sum | solution.py:44
  479.4 4.2 fusion.2
  483.7 3.7 fusion.3
  487.4 3.7 fusion.4
  495.0 9.7 %add_convert_fusion = bf16[512,3072]{1,0:T(8,128)(2,1)S(1)} fusion(f32[512,3072]{1,0:T(8,128)} %copy-done.17, f32[511,3072]{1,0:T(8,128)} %fusion.2, f32[510,3072]{1,0:T(8,128)} %fusion.3, f32[509,3072]{1,0:T(8,128)} %fusion.4, f32[3072]{0:T(1024)S(1)} %copy-done.47), kind=kLoop, calls=%fused_computation.16 | loop fusion | flops 7864320 | bytes 28250112 | tf_op jit(solution)/shard_map/convert_element_type | solution.py:543
  504.8 7.8 concatenate.55
  512.5 10.5 %convolution_convert_fusion.1 = bf16[1024,4736]{1,0:T(8,128)(2,1)} fusion(bf16[512,4736]{1,0:T(8,128)(2,1)} %concatenate.55, bf16[512,1024]{1,0:T(8,128)(2,1)} %param.15, f32[1024]{0:T(1024)S(1)} %copy-done.57, f32[512]{0:T(512)S(1)} %copy-done.59), kind=kOutput, calls=%fused_computation.1 | convolution fusion | flops 4973002752 | bytes 15603712 | tf_op jit(solution)/shard_map/rd,rc->dc/dot_general | solution.py:550
  524.3 11.0 %fusion.17 = (f32[1024]{0:T(1024)S(1)}, f32[512]{0:T(512)S(1)}, f32[512,1024]{1,0:T(8,128)}) fusion(bf16[512,1024]{1,0:T(8,128)(2,1)S(1)} %copy-done.29, f32[512]{0:T(512)S(1)} %copy-done.59, f32[1024]{0:T(1024)S(1)} %copy-done.57, bf16[512,4736]{1,0:T(8,128)(2,1)} %concatenate.55, bf16[1024,4736]{1,0:T(8,128)(2,1)} %all-gather.5.cloned.1.call-done), kind=kOutput, calls=%fused_computation.58 | convolution fusion | flops 4969724416 | bytes 17707008 | tf_op jit(solution)/shard_map/rc,dc->rd/dot_general | solution.py:553
  535.4 42.5 %psum.7 = f32[14604]{0:T(1024)S(1)} all-reduce(f32[14604]{0:T(1024)S(1)} %constant_dynamic-update-slice_fusion.16), channel_id=1, replica_groups=mesh['fsdp'=32] {'fsdp'}, use_global_device_ids=true, to_apply=%region_22.23 | all-reduce | flops 14604 | bytes 116832 | tf_op jit(solution)/shard_map/psum | solution.py:564
  580.5 3.6 fusion.19
  584.1 6.8 multiply_convert_fusion.3
  590.9 82.4 %reduce-scatter.3.cloned.1.call-done = bf16[32,4736]{1,0:T(8,128)(2,1)} async-done(((bf16[1024,4736]{1,0:T(8,128)(2,1)}), bf16[32,4736]{1,0:T(8,128)(2,1)}) %reduce-scatter.3.cloned.1.call-update) | async-done | bytes 303120 | tf_op jit(solution)/shard_map/reduce_scatter | solution.py:558
  678.0 214.0 %reduce-scatter.5.cloned.1.call-done = bf16[624,512]{1,0:T(8,128)(2,1)} async-done(((bf16[19968,512]{1,0:T(8,128)(2,1)}), bf16[624,512]{1,0:T(8,128)(2,1)}) %reduce-scatter.5.cloned.1.call-update) | async-done | bytes 638992 | tf_op jit(solution)/shard_map/reduce_scatter | solution.py:525
  (303 shorter events, 103.7 us)
Async XLA Ops:
  7.2 97.8 %copy-start.27 = (bf16[512,1024]{1,0:T(8,128)(2,1)S(1)}, bf16[512,1024]{1,0:T(8,128)(2,1)}, u32[]{:S(2)}) copy-start(bf16[512,1024]{1,0:T(8,128)(2,1)} %param.15) | copy-start | bytes 3145732
  7.2 98.1 %copy-start.72 = (f32[2,6]{1,0:T(2,128)S(1)}, f32[2,6]{1,0:T(2,128)}, u32[]{:S(2)}) copy-start(f32[2,6]{1,0:T(2,128)} %param.21) | copy-start | bytes 148
  7.2 91.2 %all-gather.5.cloned.1.call-start = ((), (), s32[]{:S(2)}) async-start(), calls=%async_computation.2 | async-start | bytes 10002432 | tf_op jit(solution)/shard_map/all_gather | solution.py:452
  12.3 209.2 %all-gather.9.cloned.1.call-start = ((), (), s32[]{:S(2)}) async-start(), calls=%async_computation.6 | async-start | bytes 9191424 | tf_op jit(solution)/shard_map/all_gather | solution.py:458
  98.4 175.0 %all-gather.7.cloned.1.call-start = ((), (), s32[]{:S(2)}) async-start(), calls=%async_computation.3 | async-start | bytes 11894784 | tf_op jit(solution)/shard_map/all_gather | solution.py:459
  99.2 574.1 %reduce-scatter.3.cloned.1.call-start = ((), (), s32[]{:S(2)}) async-start(), calls=%async_computation.4 | async-start | bytes 10002432 | tf_op jit(solution)/shard_map/reduce_scatter | solution.py:558
  102.3 28.7 %copy-start.64 = (pred[512]{0:T(512)(128)(4,1)}, pred[512]{0:T(512)(128)(4,1)S(1)}, u32[]{:S(2)}) copy-start(pred[512]{0:T(512)(128)(4,1)S(1)} %get-tuple-element.212) | copy-start | bytes 1540
  102.3 28.7 %copy-start.66 = (pred[512]{0:T(512)(128)(4,1)}, pred[512]{0:T(512)(128)(4,1)S(1)}, u32[]{:S(2)}) copy-start(pred[512]{0:T(512)(128)(4,1)S(1)} %get-tuple-element.213) | copy-start | bytes 1540
  102.3 28.7 %copy-start.68 = (pred[512]{0:T(512)(128)(4,1)}, pred[512]{0:T(512)(128)(4,1)S(1)}, u32[]{:S(2)}) copy-start(pred[512]{0:T(512)(128)(4,1)S(1)} %get-tuple-element.214) | copy-start | bytes 1540
  105.3 10.1 %copy-start.54 = (f32[512]{0:T(512)}, f32[512]{0:T(512)S(1)}, u32[]{:S(2)}) copy-start(f32[512]{0:T(512)S(1)} %fusion.20) | copy-start | bytes 6148
  105.3 48.6 %copy-start.60 = (f32[6]{0:T(128)}, f32[6]{0:T(128)S(1)}, u32[]{:S(2)}) copy-start(f32[6]{0:T(128)S(1)} %get-tuple-element.217) | copy-start | bytes 76
  105.3 48.5 %copy-start.62 = (f32[6]{0:T(128)}, f32[6]{0:T(128)S(1)}, u32[]{:S(2)}) copy-start(f32[6]{0:T(128)S(1)} %get-tuple-element.218) | copy-start | bytes 76
  105.3 10.1 %copy-start.58 = (f32[512]{0:T(512)}, f32[512]{0:T(512)S(1)}, u32[]{:S(2)}) copy-start(f32[512]{0:T(512)S(1)} %fusion.55) | copy-start | bytes 6148
  106.8 8.6 copy-start.56
  115.4 7.5 copy-start.18
  130.9 13.4 %copy-start.46 = (f32[3072]{0:T(1024)}, f32[3072]{0:T(1024)S(1)}, u32[]{:S(2)}) copy-start(f32[3072]{0:T(1024)S(1)} %get-tuple-element.152) | copy-start | bytes 36868
  130.9 13.4 %copy-start.48 = (f32[3072]{0:T(1024)}, f32[3072]{0:T(1024)S(1)}, u32[]{:S(2)}) copy-start(f32[3072]{0:T(1024)S(1)} %get-tuple-element.153) | copy-start | bytes 36868
  130.9 13.4 %copy-start.50 = (f32[3072]{0:T(1024)}, f32[3072]{0:T(1024)S(1)}, u32[]{:S(2)}) copy-start(f32[3072]{0:T(1024)S(1)} %get-tuple-element.154) | copy-start | bytes 36868
  130.9 13.4 %copy-start.52 = (f32[3072]{0:T(1024)}, f32[3072]{0:T(1024)S(1)}, u32[]{:S(2)}) copy-start(f32[3072]{0:T(1024)S(1)} %get-tuple-element.155) | copy-start | bytes 36868
  149.3 8.5 copy-start.22
  153.8 4.0 copy-start.26
  160.5 35.2 %copy-start.5 = (bf16[512,768]{1,0:T(8,128)(2,1)}, bf16[512,768]{1,0:T(8,128)(2,1)S(1)}, u32[]{:S(2)}) copy-start(bf16[512,768]{1,0:T(8,128)(2,1)S(1)} %get-tuple-element.186.k_ref) | copy-start | bytes 2359300
  160.5 35.2 %copy-start.7 = (bf16[512,768]{1,0:T(8,128)(2,1)}, bf16[512,768]{1,0:T(8,128)(2,1)S(1)}, u32[]{:S(2)}) copy-start(bf16[512,768]{1,0:T(8,128)(2,1)S(1)} %get-tuple-element.187.q_ref) | copy-start | bytes 2359300
  223.7 7.0 copy-start.30
  223.7 7.0 copy-start.28
  223.8 7.0 copy-start.36
  230.8 55.2 %slice-start = ((s8[5767168]{0:T(1024)(128)(4,1)}), s8[1572864]{0:T(1024)(128)(4,1)S(1)}, s32[]{:S(2)}) async-start(s8[5767168]{0:T(1024)(128)(4,1)} %bitcast.130), calls=%async_computation.7 | async-start | bytes 3145728
  273.4 12.6 %slice-start.1 = ((s8[5767168]{0:T(1024)(128)(4,1)}), s8[4194304]{0:T(1024)(128)(4,1)S(1)}, s32[]{:S(2)}) async-start(s8[5767168]{0:T(1024)(128)(4,1)} %bitcast.130), calls=%async_computation.8 | async-start | bytes 8388608
  273.4 12.6 %copy-start.39 = (bf16[512,1024]{1,0:T(8,128)(2,1)S(1)}, bf16[512,1024]{1,0:T(8,128)(2,1)}, u32[]{:S(2)}) copy-start(bf16[512,1024]{1,0:T(8,128)(2,1)} %param.29) | copy-start | bytes 3145732
  286.0 12.3 %copy-start.32 = (f32[512,1024]{1,0:T(8,128)S(1)}, f32[512,1024]{1,0:T(8,128)}, u32[]{:S(2)}) copy-start(f32[512,1024]{1,0:T(8,128)} %get-tuple-element.220) | copy-start | bytes 6291460
  298.3 9.4 %copy-start.33 = (f32[512,1024]{1,0:T(8,128)S(1)}, f32[512,1024]{1,0:T(8,128)}, u32[]{:S(2)}) copy-start(f32[512,1024]{1,0:T(8,128)} %get-tuple-element.220) | copy-start | bytes 6291460
  321.0 6.7 copy-start.40
  357.0 8.4 copy-start.23
  441.4 4.8 copy-start.43
  462.0 3.8 copy-start.65
  462.0 3.8 copy-start.67
  465.7 13.7 %copy-start.53 = (f32[3072]{0:T(1024)S(1)}, f32[3072]{0:T(1024)}, u32[]{:S(2)}) copy-start(f32[3072]{0:T(1024)} %copy-done.52) | copy-start | bytes 36868
  465.7 13.7 %copy-start.76 = (pred[511]{0:T(512)(128)(4,1)S(1)}, pred[511]{0:T(512)(128)(4,1)}, u32[]{:S(2)}) copy-start(pred[511]{0:T(512)(128)(4,1)} %slice.316) | copy-start | bytes 1537
  479.4 8.0 copy-start.17
  479.4 4.2 copy-start.51
  479.4 4.2 copy-start.75
  491.1 3.8 copy-start.47
  504.7 7.8 copy-start.57
  504.8 7.8 copy-start.59
  523.1 368.9 %reduce-scatter.5.cloned.1.call-start = ((), (), s32[]{:S(2)}) async-start(), calls=%async_computation.5 | async-start | bytes 21086208 | tf_op jit(solution)/shard_map/reduce_scatter | solution.py:525
  524.3 11.0 %copy-start.71 = (f32[1024]{0:T(1024)S(1)}, f32[1024]{0:T(1024)}, u32[]{:S(2)}) copy-start(f32[1024]{0:T(1024)} %get-tuple-element.148) | copy-start | bytes 12292
  524.3 56.1 %copy-start.55 = (f32[512]{0:T(512)S(1)}, f32[512]{0:T(512)}, u32[]{:S(2)}) copy-start(f32[512]{0:T(512)} %copy-done.54) | copy-start | bytes 6148
  524.3 56.1 %copy-start.24 = (f32[512,1024]{1,0:T(8,128)S(1)}, f32[512,1024]{1,0:T(8,128)}, u32[]{:S(2)}) copy-start(f32[512,1024]{1,0:T(8,128)} %get-tuple-element.160) | copy-start | bytes 6291460
  (40 other events, 96.5 us)
Sparse Core Ops, SparseCore 0:
  12.4 85.9 all-gather.4
  101.8 78.2 all-gather.8
  183.5 89.8 all-gather.6
  523.2 150.0 reduce-scatter.2
  680.7 211.2 reduce-scatter.4
